TPU v7x, 32 devices: a whole 2x2x4 slice. The times are simulated.
32 devices in a mesh: grp: 2 (over y), ev: 2 (over x), loc: 8 (over z, core).
Axes of the slice: x: 2, y: 2, z: 4, core: 2. Of those that a mesh axis runs over, the one named last changes fastest.
Arguments:
- intensity_bin: int32 [256, 16384], P('ev', ('grp', 'loc')), parts along dimension 1, may hold values from 0 to 62
- bin_fraction: bfloat16 [256, 16384], P('ev', ('grp', 'loc')), parts along dimension 1, may hold values from 0 to 1
- footprint_mask: int32 [256, 128], P('ev', ('grp', 'loc')), parts along dimension 1, may hold values 0 or 1
- location_contract: int32 [16384], P(('grp', 'loc')), parts along dimension 0, may hold values from 0 to 2047
- location_class: int32 [16384], P(('grp', 'loc')), parts along dimension 0, may hold values from 0 to 127
- exposure: float32 [16384], P(('grp', 'loc')), parts along dimension 0, may hold values from 0.32 to 3.2
- curves: float32 [128, 64], replicated, may hold values from 0 to 1
- event_year: int32 [256], P('ev'), may hold values from 0 to 127
- occ_retention: float32 [4096], P('grp'), parts along dimension 0, may hold values from 0.2 to 0.8
- occ_limit: float32 [4096], P('grp'), parts along dimension 0, may hold values from 0.8 to 2.5
- agg_retention: float32 [4096], P('grp'), parts along dimension 0, may hold values from 0.125 to 0.375
- agg_limit: float32 [4096], P('grp'), parts along dimension 0, may hold values from 0.375 to 1
Outputs:
- annual: float32 [4096, 128], P(('grp', 'loc'), 'ev'), parts along dimension 0
- year_mean: float32 [256], P(('grp', 'ev')), parts along dimension 0
There are 2 independent parts, one for each index of `grp`. A program takes and returns all parts, laid end to end along the dimension named above; an argument that names none is the same for every part. Nothing has to cross between parts.
All inputs are finite; a program needn't handle non-finite values. No bound on the sum of `footprint_mask` on one device may be relied on, other than what follows from the above.
Results may differ from a plain program's by a relative error of at most 0.0016.
Values sent between devices are 32-bit elements; how exact they have to be, the bound alone decides.
A program may use at most 64 MiB of HBM per device.

v0:
```python
import math

import jax
import jax.numpy as jnp
from jax import lax
from jax.sharding import PartitionSpec as P

YR_DEV = 64


def local(
    intensity_bin,
    bin_fraction,
    footprint_mask,
    location_contract,
    location_class,
    exposure,
    curves,
    event_year,
    occ_retention,
    occ_limit,
    agg_retention,
    agg_limit,
):
    ev_rows, loc_cols = intensity_bin.shape
    curve_count, knot_count = curves.shape
    contract_count = occ_retention.shape[0]
    share = contract_count // lax.axis_size("loc")
    class_onehot = (
        location_class[:, None] == jnp.arange(curve_count, dtype=jnp.int32)[None, :]
    ).astype(jnp.float32)
    knot_table = lax.dot_general(
        curves,
        class_onehot,
        (((0,), (1,)), ((), ())),
        precision=lax.Precision.HIGHEST,
        preferred_element_type=jnp.float32,
    )
    knot_index = jnp.arange(knot_count, dtype=jnp.int32)[None, :, None]
    rows_step = math.gcd(ev_rows, 16)
    step_count = ev_rows // rows_step
    mask_cols = footprint_mask.shape[1]

    def damage_rows(pieces):
        bins, frac, mask = pieces
        weight = frac.astype(jnp.float32)[:, None, :]
        bins_wide = bins[:, None, :]
        hats = jnp.where(bins_wide == knot_index, 1.0 - weight, 0.0) + jnp.where(
            bins_wide + 1 == knot_index, weight, 0.0
        )
        damage = jnp.sum(hats * knot_table[None, :, :], axis=1)
        blocks = (
            damage.reshape(rows_step, mask_cols, loc_cols // mask_cols)
            * mask.astype(jnp.float32)[:, :, None]
        )
        return (blocks.reshape(rows_step, loc_cols) * exposure[None, :]).astype(jnp.bfloat16)

    loss = lax.map(
        damage_rows,
        (
            intensity_bin.reshape(step_count, rows_step, loc_cols),
            bin_fraction.reshape(step_count, rows_step, loc_cols),
            footprint_mask.reshape(step_count, rows_step, mask_cols),
        ),
    ).reshape(ev_rows, loc_cols)
    first = lax.axis_index("loc") * share
    width = math.gcd(lax.axis_size("loc") * share, 256)
    pieces = lax.axis_size("loc") * share // width

    def one_piece(which):
        member = (
            location_contract[:, None]
            == which * width + jnp.arange(width, dtype=jnp.int32)[None, :]
        ).astype(jnp.bfloat16)
        return lax.dot_general(
            member, loss, (((0,), (1,)), ((), ())), preferred_element_type=jnp.float32
        )

    totals = lax.psum_scatter(
        lax.map(one_piece, jnp.arange(pieces, dtype=jnp.int32)).reshape(
            lax.axis_size("loc") * share, ev_rows
        ),
        "loc",
        scatter_dimension=0,
        tiled=True,
    )
    own_ret = lax.dynamic_slice_in_dim(occ_retention, first, share, 0)
    own_lim = lax.dynamic_slice_in_dim(occ_limit, first, share, 0)
    own_aret = lax.dynamic_slice_in_dim(agg_retention, first, share, 0)
    own_alim = lax.dynamic_slice_in_dim(agg_limit, first, share, 0)
    occurrence = jnp.minimum(jnp.maximum(totals - own_ret[:, None], 0.0), own_lim[:, None])
    year_count = YR_DEV * lax.axis_size("ev")
    year_onehot = (event_year[:, None] == jnp.arange(year_count, dtype=jnp.int32)[None, :]).astype(
        jnp.float32
    )
    partial_years = jnp.dot(
        occurrence, year_onehot, precision=lax.Precision.HIGHEST, preferred_element_type=jnp.float32
    )
    yearly = lax.psum_scatter(partial_years, "ev", scatter_dimension=1, tiled=True)
    annual = jnp.minimum(jnp.maximum(yearly - own_aret[:, None], 0.0), own_alim[:, None])
    year_mean = lax.psum(jnp.sum(annual, axis=0), "loc") / contract_count
    return (annual, year_mean)


def solution(mesh):
    in_specs = (
        P("ev", ("grp", "loc")),
        P("ev", ("grp", "loc")),
        P("ev", ("grp", "loc")),
        P(("grp", "loc")),
        P(("grp", "loc")),
        P(("grp", "loc")),
        P(),
        P("ev"),
        P("grp"),
        P("grp"),
        P("grp"),
        P("grp"),
    )
    out_specs = (P(("grp", "loc"), "ev"), P(("grp", "ev")))
    return jax.shard_map(local, mesh=mesh, in_specs=in_specs, out_specs=out_specs, check_vma=False)
```

profile of v0, /device:TPU:0, one launch (start us, length us, event | category | flops | bytes accessed | tf_op | source)
XLA Modules:
  0.0 134.4 jit_solution(8424766924364381948)
XLA Ops:
  7.2 0.8 reshape.108
  8.0 1.2 convolution_bitcast_fusion.1
  9.2 34.5 %while.23 = (s32[]{:T(128)}, bf16[8,16,1024]{2,1,0:T(8,128)(2,1)S(1)}, s32[8,16,1024]{2,1,0:T(8,128)}, bf16[8,16,1024]{2,1,0:T(8,128)(2,1)}, f32[64,1024]{1,0:T(...) while((s32[]{:T(128)}, bf16[8,16,1024]{2,1,0:T(8,128)(2,1)S(1)}, ...), condition=%wide.region_2.3_spmd.clone.clone, body=%wide.region_0.2_spmd.clone.clone.sunk | while | flops 7438466 | bytes 1367693 | solution.py:58
  9.5 0.8 bitcast_convert_fusion.2
  10.2 0.8 broadcast_add_fusion.2
  11.1 0.8 broadcast_subtract_fusion.2
  11.9 1.6 %multiply_reduce_fusion.2 = f32[16,1024]{1,0:T(8,128)S(1)} fusion(f32[64,1024]{1,0:T(8,128)S(1)} %get-tuple-element.252, f32[16,1024]{1,0:T(8,128)S(1)} %bitcast_convert_fusion.2, s32[16,1024]{1,0:T(8,128)S(1)} %get-tuple-element.230, f32[16,1024]{1,0:T(8,128)S(1)} %broadcast_subtract_fusion.2, s32[16,1024]{1,0:T(8,128)S(1)} %get-tuple-element.231), kind=kLoop, calls=%fused_computation.9.clone.1 | loop fusion | flops 7323648 | bytes 589824 | tf_op jit(solution)/shard_map/while/body/eval_jaxpr/reduce_sum | solution.py:51
  13.7 0.1 mul.94
  13.8 0.8 bitcast_convert_fusion.2
  14.6 0.8 broadcast_add_fusion.2
  15.4 0.8 broadcast_subtract_fusion.2
  16.2 1.6 %multiply_reduce_fusion.2 = f32[16,1024]{1,0:T(8,128)S(1)} fusion(f32[64,1024]{1,0:T(8,128)S(1)} %get-tuple-element.252, f32[16,1024]{1,0:T(8,128)S(1)} %bitcast_convert_fusion.2, s32[16,1024]{1,0:T(8,128)S(1)} %get-tuple-element.230, f32[16,1024]{1,0:T(8,128)S(1)} %broadcast_subtract_fusion.2, s32[16,1024]{1,0:T(8,128)S(1)} %get-tuple-element.231), kind=kLoop, calls=%fused_computation.9.clone.1 | loop fusion | flops 7323648 | bytes 589824 | tf_op jit(solution)/shard_map/while/body/eval_jaxpr/reduce_sum | solution.py:51
  18.0 0.1 mul.94
  18.1 0.8 bitcast_convert_fusion.2
  18.9 0.8 broadcast_add_fusion.2
  19.7 0.8 broadcast_subtract_fusion.2
  20.5 1.6 %multiply_reduce_fusion.2 = f32[16,1024]{1,0:T(8,128)S(1)} fusion(f32[64,1024]{1,0:T(8,128)S(1)} %get-tuple-element.252, f32[16,1024]{1,0:T(8,128)S(1)} %bitcast_convert_fusion.2, s32[16,1024]{1,0:T(8,128)S(1)} %get-tuple-element.230, f32[16,1024]{1,0:T(8,128)S(1)} %broadcast_subtract_fusion.2, s32[16,1024]{1,0:T(8,128)S(1)} %get-tuple-element.231), kind=kLoop, calls=%fused_computation.9.clone.1 | loop fusion | flops 7323648 | bytes 589824 | tf_op jit(solution)/shard_map/while/body/eval_jaxpr/reduce_sum | solution.py:51
  22.4 0.8 bitcast_convert_fusion.2
  23.2 0.8 broadcast_add_fusion.2
  24.0 0.8 broadcast_subtract_fusion.2
  24.8 1.6 %multiply_reduce_fusion.2 = f32[16,1024]{1,0:T(8,128)S(1)} fusion(f32[64,1024]{1,0:T(8,128)S(1)} %get-tuple-element.252, f32[16,1024]{1,0:T(8,128)S(1)} %bitcast_convert_fusion.2, s32[16,1024]{1,0:T(8,128)S(1)} %get-tuple-element.230, f32[16,1024]{1,0:T(8,128)S(1)} %broadcast_subtract_fusion.2, s32[16,1024]{1,0:T(8,128)S(1)} %get-tuple-element.231), kind=kLoop, calls=%fused_computation.9.clone.1 | loop fusion | flops 7323648 | bytes 589824 | tf_op jit(solution)/shard_map/while/body/eval_jaxpr/reduce_sum | solution.py:51
  26.7 0.8 bitcast_convert_fusion.2
  27.5 0.8 broadcast_add_fusion.2
  28.3 0.8 broadcast_subtract_fusion.2
  29.1 1.6 %multiply_reduce_fusion.2 = f32[16,1024]{1,0:T(8,128)S(1)} fusion(f32[64,1024]{1,0:T(8,128)S(1)} %get-tuple-element.252, f32[16,1024]{1,0:T(8,128)S(1)} %bitcast_convert_fusion.2, s32[16,1024]{1,0:T(8,128)S(1)} %get-tuple-element.230, f32[16,1024]{1,0:T(8,128)S(1)} %broadcast_subtract_fusion.2, s32[16,1024]{1,0:T(8,128)S(1)} %get-tuple-element.231), kind=kLoop, calls=%fused_computation.9.clone.1 | loop fusion | flops 7323648 | bytes 589824 | tf_op jit(solution)/shard_map/while/body/eval_jaxpr/reduce_sum | solution.py:51
  31.0 0.8 bitcast_convert_fusion.2
  31.8 0.8 broadcast_add_fusion.2
  32.6 0.8 broadcast_subtract_fusion.2
  33.4 1.6 %multiply_reduce_fusion.2 = f32[16,1024]{1,0:T(8,128)S(1)} fusion(f32[64,1024]{1,0:T(8,128)S(1)} %get-tuple-element.252, f32[16,1024]{1,0:T(8,128)S(1)} %bitcast_convert_fusion.2, s32[16,1024]{1,0:T(8,128)S(1)} %get-tuple-element.230, f32[16,1024]{1,0:T(8,128)S(1)} %broadcast_subtract_fusion.2, s32[16,1024]{1,0:T(8,128)S(1)} %get-tuple-element.231), kind=kLoop, calls=%fused_computation.9.clone.1 | loop fusion | flops 7323648 | bytes 589824 | tf_op jit(solution)/shard_map/while/body/eval_jaxpr/reduce_sum | solution.py:51
  35.3 0.8 bitcast_convert_fusion.2
  36.1 0.8 broadcast_add_fusion.2
  36.9 0.8 broadcast_subtract_fusion.2
  37.7 1.6 %multiply_reduce_fusion.2 = f32[16,1024]{1,0:T(8,128)S(1)} fusion(f32[64,1024]{1,0:T(8,128)S(1)} %get-tuple-element.252, f32[16,1024]{1,0:T(8,128)S(1)} %bitcast_convert_fusion.2, s32[16,1024]{1,0:T(8,128)S(1)} %get-tuple-element.230, f32[16,1024]{1,0:T(8,128)S(1)} %broadcast_subtract_fusion.2, s32[16,1024]{1,0:T(8,128)S(1)} %get-tuple-element.231), kind=kLoop, calls=%fused_computation.9.clone.1 | loop fusion | flops 7323648 | bytes 589824 | tf_op jit(solution)/shard_map/while/body/eval_jaxpr/reduce_sum | solution.py:51
  39.6 0.8 bitcast_convert_fusion.2
  40.4 0.8 broadcast_add_fusion.2
  41.3 0.8 broadcast_subtract_fusion.2
  42.0 1.6 %multiply_reduce_fusion.2 = f32[16,1024]{1,0:T(8,128)S(1)} fusion(f32[64,1024]{1,0:T(8,128)S(1)} %get-tuple-element.252, f32[16,1024]{1,0:T(8,128)S(1)} %bitcast_convert_fusion.2, s32[16,1024]{1,0:T(8,128)S(1)} %get-tuple-element.230, f32[16,1024]{1,0:T(8,128)S(1)} %broadcast_subtract_fusion.2, s32[16,1024]{1,0:T(8,128)S(1)} %get-tuple-element.231), kind=kLoop, calls=%fused_computation.9.clone.1 | loop fusion | flops 7323648 | bytes 589824 | tf_op jit(solution)/shard_map/while/body/eval_jaxpr/reduce_sum | solution.py:51
  43.7 19.5 %while.22 = (s32[]{:T(128)}, f32[8,256,128]{2,1,0:T(8,128)}, s32[1024]{0:T(1024)S(1)}, s32[8]{0:T(128)S(1)}, bf16[128,1024]{1,0:T(8,128)(2,1)S(1)}, /*index=5*/s32[]{:T(128)}, s32[1]{0:T(128)}) while((s32[]{:T(128)}, f32[8,256,128]{2,1,0:T(8,128)}, s32[1024]{0:T(1024)S(1)}, s32[8]{0:T(128)S(1)}, bf16[128,1024]{1,0:T(8,128)(2,1)S(1)}, ...), condition=%wide.region_4.5_spmd, body=%wide.region_3.4_spmd.sunk | while | flops 67633408 | bytes 399477 | solution.py:80
  43.7 0.6 dynamic_slice.48
  45.0 1.2 fusion.25
  46.2 0.6 dynamic_slice.48
  47.4 1.2 fusion.25
  48.6 0.6 dynamic_slice.48
  49.9 1.2 fusion.25
  51.1 0.6 dynamic_slice.48
  52.3 1.2 fusion.25
  53.5 0.6 dynamic_slice.48
  54.7 1.2 fusion.25
  55.9 0.6 dynamic_slice.48
  57.2 1.2 fusion.25
  58.3 0.6 dynamic_slice.48
  59.6 1.2 fusion.25
  60.8 0.6 dynamic_slice.48
  62.0 1.2 fusion.25
  63.3 0.8 dynamic_slice.29
  64.1 0.8 dynamic_slice.28
  64.8 33.6 %reduce-scatter.3.cloned.1.call-done = f32[256,128]{1,0:T(8,128)} async-done(((f32[2048,128]{1,0:T(8,128)}), f32[256,128]{1,0:T(8,128)}) %reduce-scatter.3.cloned.1.call-update) | async-done | bytes 131088 | tf_op jit(solution)/shard_map/reduce_scatter | solution.py:79
  98.4 1.9 %fusion.9 = f32[256,128]{0,1:T(8,128)} fusion(f32[256,128]{1,0:T(8,128)} %reduce-scatter.3.cloned.1.call-done, f32[256]{0:T(256)S(1)} %dynamic_slice.29, f32[256]{0:T(256)S(1)} %dynamic_slice.28, s32[128]{0:T(128)S(1)} %copy-done.2), kind=kOutput, calls=%fused_computation.23 | convolution fusion | flops 50446336 | bytes 264704 | tf_op jit(solution)/shard_map/dot_general | solution.py:96
  100.4 0.8 dynamic_slice.31
  101.1 0.8 dynamic_slice.30
  101.9 7.3 %reduce-scatter.5.cloned.1.call-done = f32[256,64]{0,1:T(8,128)} async-done(((f32[256,128]{0,1:T(8,128)}), f32[256,64]{0,1:T(8,128)}) %reduce-scatter.5.cloned.1.call-update) | async-done | bytes 65552 | tf_op jit(solution)/shard_map/reduce_scatter | solution.py:99
  109.2 1.6 %fusion.18 = (f32[64]{0:T(128)S(1)}, f32[256,64]{0,1:T(8,128)}) fusion(f32[256]{0:T(256)S(1)} %dynamic_slice.31, f32[256,64]{0,1:T(8,128)} %reduce-scatter.5.cloned.1.call-done, f32[256]{0:T(256)S(1)} %dynamic_slice.30), kind=kLoop, calls=%fused_computation.35 | loop fusion | flops 65472 | bytes 133376 | tf_op jit(solution)/shard_map/reduce_sum | solution.py:101
  110.8 16.3 %psum.7 = f32[64]{0:T(128)S(1)} all-reduce(f32[64]{0:T(128)S(1)} %get-tuple-element.152), channel_id=1, replica_groups=mesh['grp'=2,'ev'=2,'loc'=8] {'loc'}, use_global_device_ids=true, to_apply=%region_8.9 | all-reduce | flops 64 | bytes 512 | tf_op jit(solution)/shard_map/psum | solution.py:101
  127.1 0.5 broadcast_multiply_fusion
  (83 shorter events, 1.7 us)
Async XLA Ops:
  7.2 0.8 copy-start
  7.2 91.2 %reduce-scatter.3.cloned.1.call-start = ((), (), s32[]{:S(2)}) async-start(), calls=%async_computation.2 | async-start | bytes 1179648 | tf_op jit(solution)/shard_map/reduce_scatter | solution.py:79
  9.2 34.5 %copy-start.3 = (s32[1024]{0:T(1024)S(1)}, s32[1024]{0:T(1024)}, u32[]{:S(2)}) copy-start(s32[1024]{0:T(1024)} %param.19) | copy-start | bytes 12292
  9.3 4.3 %copy-start.1 = (f32[1024]{0:T(1024)S(1)}, f32[1024]{0:T(1024)}, u32[]{:S(2)}) copy-start(f32[1024]{0:T(1024)} %get-tuple-element.254) | copy-start | bytes 12292 | tf_op jit(solution)/shard_map/while
  13.6 4.3 %copy-start.1 = (f32[1024]{0:T(1024)S(1)}, f32[1024]{0:T(1024)}, u32[]{:S(2)}) copy-start(f32[1024]{0:T(1024)} %get-tuple-element.254) | copy-start | bytes 12292 | tf_op jit(solution)/shard_map/while
  17.9 4.3 %copy-start.1 = (f32[1024]{0:T(1024)S(1)}, f32[1024]{0:T(1024)}, u32[]{:S(2)}) copy-start(f32[1024]{0:T(1024)} %get-tuple-element.254) | copy-start | bytes 12292 | tf_op jit(solution)/shard_map/while
  22.2 4.3 %copy-start.1 = (f32[1024]{0:T(1024)S(1)}, f32[1024]{0:T(1024)}, u32[]{:S(2)}) copy-start(f32[1024]{0:T(1024)} %get-tuple-element.254) | copy-start | bytes 12292 | tf_op jit(solution)/shard_map/while
  26.5 4.3 %copy-start.1 = (f32[1024]{0:T(1024)S(1)}, f32[1024]{0:T(1024)}, u32[]{:S(2)}) copy-start(f32[1024]{0:T(1024)} %get-tuple-element.254) | copy-start | bytes 12292 | tf_op jit(solution)/shard_map/while
  30.8 4.3 %copy-start.1 = (f32[1024]{0:T(1024)S(1)}, f32[1024]{0:T(1024)}, u32[]{:S(2)}) copy-start(f32[1024]{0:T(1024)} %get-tuple-element.254) | copy-start | bytes 12292 | tf_op jit(solution)/shard_map/while
  35.1 4.3 %copy-start.1 = (f32[1024]{0:T(1024)S(1)}, f32[1024]{0:T(1024)}, u32[]{:S(2)}) copy-start(f32[1024]{0:T(1024)} %get-tuple-element.254) | copy-start | bytes 12292 | tf_op jit(solution)/shard_map/while
  39.4 4.3 %copy-start.1 = (f32[1024]{0:T(1024)S(1)}, f32[1024]{0:T(1024)}, u32[]{:S(2)}) copy-start(f32[1024]{0:T(1024)} %get-tuple-element.254) | copy-start | bytes 12292 | tf_op jit(solution)/shard_map/while
  63.2 35.2 %copy-start.2 = (s32[128]{0:T(128)S(1)}, s32[128]{0:T(128)}, u32[]{:S(2)}) copy-start(s32[128]{0:T(128)} %param.23) | copy-start | bytes 1540
  63.2 45.9 %reduce-scatter.5.cloned.1.call-start = ((), (), s32[]{:S(2)}) async-start(), calls=%async_computation.3 | async-start | bytes 196608 | tf_op jit(solution)/shard_map/reduce_scatter | solution.py:99
Sparse Core Ops, SparseCore 0:
  63.4 35.0 reduce-scatter.2
  100.6 8.4 reduce-scatter.4
where the time goes:
time: 136 us; the launch traced here: 134 us
  waiting for transfers between devices  40.9 us (30%)
  other arithmetic  34.6 us (25%)
  blocking collectives  16.3 us (12%)
  between operations  14.1 us (10%)
  matrix products  12.6 us (9%)
  local copies, waits for them, and re-layouts  9.98 us (7%)
  loops' own time  5.83 us (4%)
    reduce_scatter x1, waiting for transfers between devices, local(): lax.psum_scatter(lax.map(one_piece, jnp.arange(pieces, dtype=jnp.int32))....  33.6 us
    psum x1, blocking collectives, local(): year_mean = lax.psum(jnp.sum(annual, axis=0), 'loc') / contract_count  16.3 us
    reduce_sum x8, other arithmetic, damage_rows(): damage = jnp.sum(hats * knot_table[None, :, :], axis=1)  13.1 us
    dot_general x8, matrix products, one_piece(): lax.dot_general(member, loss, (((0,), (1,)), ((), ())), preferred_element...  9.5 us
    reduce_scatter x1, waiting for transfers between devices, local(): lax.psum_scatter(partial_years, 'ev', scatter_dimension=1, tiled=True)  7.3 us
    add x8, other arithmetic, damage_rows(): bins_wide + 1 == knot_index  6.79 us
    sub x8, other arithmetic, damage_rows(): 1.0 - weight  6.17 us
    convert_element_type x8, other arithmetic, damage_rows(): weight = frac.astype(jnp.float32)[:, None, :]  6.16 us
  transfers between devices with their start and end apart: 2, of which 2 were waited for; matrix products, arithmetic and copies ran while one was open for 2% of the time, Pallas kernels for 0%

commit v1 on v0

v1 whole, which is shorter than its diff:
```python
import functools

import jax
import jax.numpy as jnp
from jax import lax
from jax.experimental import pallas as pl
from jax.experimental.pallas import tpu as pltpu
from jax.sharding import PartitionSpec as P

YR_DEV = 64
CORES = 2
LANES = 128
MESH = pl.DeviceIdType.MESH
F32, BF16, I32 = jnp.float32, jnp.bfloat16, jnp.int32

NT = (((1,), (1,)), ((), ()))
TN = (((0,), (0,)), ((), ()))


def iota(shape, axis):
    return lax.broadcasted_iota(I32, shape, axis)


def split(x):
    high = x.astype(BF16)
    return high, (x - high.astype(F32)).astype(BF16)


def kernel(
    n_loc,
    n_ev,
    bins_ref,
    frac_ref,
    mask_ref,
    contract_ref,
    class_ref,
    expo_ref,
    curves_ref,
    year_ref,
    oret_ref,
    olim_ref,
    aret_ref,
    alim_ref,
    annual_ref,
    mean_ref,
    spread,
    psib,
    own,
    sibr,
    upr,
    dnr,
    ybuf,
    yrecv,
    msend,
    mrecv,
    sib_send,
    sib_recv,
    up_send,
    up_recv,
    dn_send,
    dn_recv,
    y_send,
    y_recv,
    m_send,
    m_recv,
):
    nz = n_loc // CORES
    events, locs = bins_ref.shape
    blocks = mask_ref.shape[1]
    wide = locs // blocks
    curve_count, knots = curves_ref.shape
    share = annual_ref.shape[0]
    chip = share * CORES
    contracts = share * n_loc
    chunk = ybuf.shape[3]
    chunks = share // chunk

    me = lax.axis_index("loc")
    ev = lax.axis_index("ev")
    z, core = me // CORES, me % CORES
    other = 1 - core
    sibling = z * CORES + other

    barrier = pltpu.get_barrier_semaphore()
    for k in range(1, n_loc):
        pl.semaphore_signal(
            barrier, inc=1, device_id={"loc": lax.rem(me + k, n_loc)}, device_id_type=MESH
        )
    for k in range(1, n_ev):
        pl.semaphore_signal(
            barrier, inc=1, device_id={"ev": lax.rem(ev + k, n_ev)}, device_id_type=MESH
        )

    curves = curves_ref[...]
    steps = jnp.concatenate(
        [curves[:, 1:] - curves[:, :-1], jnp.zeros((curve_count, 1), F32)], axis=1
    )
    c_high, c_low = split(jnp.concatenate([curves, steps], axis=1))
    blank = jnp.zeros((curve_count, LANES), BF16)
    first_row = (iota((16, LANES), 0) == 0).astype(F32).astype(BF16)
    table_rhs = jnp.concatenate(
        [
            jnp.concatenate([c_high, c_high, c_low, jnp.zeros((16, LANES), BF16)], axis=0),
            jnp.concatenate([blank, blank, blank, first_row], axis=0),
        ],
        axis=1,
    )
    eye = (iota((blocks, blocks), 0) == iota((blocks, blocks), 1)).astype(F32).astype(BF16)
    keep = lax.dot_general(
        eye, mask_ref[...].astype(F32).astype(BF16), NT, preferred_element_type=F32
    )
    rows_in_chip = []
    for b in range(blocks):
        cols = pl.ds(b * wide, wide)
        contract = contract_ref[b : b + 1, :]
        where_chip = jnp.zeros_like(contract)
        for t in range(1, nz):
            where_chip += (contract >= t * chip).astype(I32)
        rows_in_chip.append(contract - where_chip * chip)
        weight = jnp.where(
            iota((curve_count, wide), 0) == class_ref[b : b + 1, :], expo_ref[b : b + 1, :], 0.0
        )
        w_high, w_low = split(weight)
        chip_rows = jnp.where(iota((16, wide), 0) == 0, where_chip.astype(F32), 0.0).astype(BF16)
        lhs = jnp.concatenate([w_high, w_low, w_high, chip_rows], axis=0)
        both = lax.dot_general(lhs, table_rhs, TN, preferred_element_type=F32)
        table, home = both[:, :LANES], both[:, LANES:]
        place = (bins_ref[:, cols].astype(F32) + frac_ref[:, cols].astype(F32)).T
        knot = place.astype(I32)
        part = place - knot.astype(F32)
        low = jnp.take_along_axis(table, knot, axis=1, mode="promise_in_bounds")
        rise = jnp.take_along_axis(table, knot + knots, axis=1, mode="promise_in_bounds")
        loss = (low + part * rise) * keep[b : b + 1, :]
        for t in range(nz):
            spread[cols, pl.ds(t * events, events)] = jnp.where(home == t, loss, 0.0).astype(BF16)

    def partial(which):
        member = jnp.concatenate(
            [
                (iota((share, wide), 0) + which * share == rows).astype(F32).astype(BF16)
                for rows in rows_in_chip
            ],
            axis=1,
        )
        return jnp.dot(member, spread[...], preferred_element_type=F32)

    sums = partial(other)
    for t in range(nz):
        psib[t] = sums[:, t * events : (t + 1) * events]

    pl.semaphore_wait(barrier, n_loc - 1 + n_ev - 1)

    def sib_copy(t):
        return pltpu.make_async_remote_copy(
            src_ref=psib.at[t],
            dst_ref=sibr.at[t],
            send_sem=sib_send.at[t],
            recv_sem=sib_recv.at[t],
            device_id={"loc": sibling},
            device_id_type=MESH,
        )

    order = []
    for t in range((nz + 1) // 2):
        order += [t] if t == nz - 1 - t else [nz - 1 - t, t]
    for t in order:
        sib_copy(t).start()

    sums = partial(core)
    for t in range(nz):
        own[t] = sums[:, t * events : (t + 1) * events]

    first = me * share

    def row_of(ref, c):
        start = first + c * chunk
        row = ref[pl.ds(start // LANES, 1), :]
        if share % LANES:
            row = pltpu.roll(
                jnp.broadcast_to(row, (8, LANES)), (LANES - start % LANES) % LANES, 1
            )[:1]
        return row[:, :chunk]

    def column_of(ref, c):
        row = jnp.broadcast_to(row_of(ref, c), (chunk, chunk))
        return jnp.sum(
            jnp.where(iota((chunk, chunk), 0) == iota((chunk, chunk), 1), row, 0.0),
            axis=1,
            keepdims=True,
        )

    orets = [column_of(oret_ref, c) for c in range(chunks)]
    olims = [column_of(olim_ref, c) for c in range(chunks)]
    year_rows = (iota((n_ev * YR_DEV, events), 0) == year_ref[...]).astype(F32).astype(BF16)
    year_rows = jnp.concatenate([year_rows, year_rows], axis=1)

    def hop(t, c, send, recv, into, step):
        rows = pl.ds(c * chunk, chunk)
        return pltpu.make_async_remote_copy(
            src_ref=own.at[t, rows],
            dst_ref=into.at[t, rows],
            send_sem=send.at[t, c],
            recv_sem=recv.at[t, c],
            device_id={"loc": me + step},
            device_id_type=MESH,
        )

    up = functools.partial(hop, send=up_send, recv=up_recv, into=upr, step=CORES)
    down = functools.partial(hop, send=dn_send, recv=dn_recv, into=dnr, step=-CORES)

    def pass_on(t, c, way, into, inner):
        rows = pl.ds(c * chunk, chunk)
        if c == 0:
            sib_copy(t).wait_recv()

        @pl.when(inner)
        def _():
            way(t, c).wait_recv()
            own[t, rows] = own[t, rows] + sibr[t, rows] + into[t, rows]

        @pl.when(jnp.logical_not(inner))
        def _():
            own[t, rows] = own[t, rows] + sibr[t, rows]

        way(t, c).start()

    for tau in range(nz - 1):
        for c in range(chunks):

            @pl.when(z <= tau)
            def _():
                pass_on(nz - 1 - tau + z, c, up, upr, z > 0)

            @pl.when(nz - 1 - z <= tau)
            def _():
                pass_on(tau - (nz - 1) + z, c, down, dnr, z < nz - 1)

    def year_copy(c, k):
        return pltpu.make_async_remote_copy(
            src_ref=ybuf.at[c, lax.rem(ev + k, n_ev)],
            dst_ref=yrecv.at[c, k - 1],
            send_sem=y_send.at[c, k - 1],
            recv_sem=y_recv.at[c, k - 1],
            device_id={"ev": lax.rem(ev + k, n_ev)},
            device_id_type=MESH,
        )

    sib_copy(z).wait_recv()
    for c in range(chunks):
        rows = pl.ds(c * chunk, chunk)
        own[z, rows] = own[z, rows] + sibr[z, rows]

        @pl.when(z > 0)
        def _():
            up(z, c).wait_recv()
            own[z, rows] = own[z, rows] + upr[z, rows]

        @pl.when(z < nz - 1)
        def _():
            down(z, c).wait_recv()
            own[z, rows] = own[z, rows] + dnr[z, rows]

        occurrence = jnp.minimum(jnp.maximum(own[z, rows] - orets[c], 0.0), olims[c])
        years = lax.dot_general(
            year_rows,
            jnp.concatenate(split(occurrence), axis=1),
            NT,
            preferred_element_type=F32,
        )
        for j in range(n_ev):
            ybuf[c, j] = years[j * YR_DEV : (j + 1) * YR_DEV]
        for k in range(1, n_ev):
            year_copy(c, k).start()

    total = jnp.zeros((1, YR_DEV), F32)
    for c in range(chunks):
        yearly = ybuf[c, ev]
        for k in range(1, n_ev):
            year_copy(c, k).wait_recv()
            yearly += yrecv[c, k - 1]
        annual = jnp.minimum(
            jnp.maximum(yearly - row_of(aret_ref, c), 0.0), row_of(alim_ref, c)
        )
        annual = annual.T
        annual_ref[c * chunk : (c + 1) * chunk, :] = annual
        total += jnp.sum(annual, axis=0, keepdims=True)

    msend[:, :YR_DEV] = jnp.broadcast_to(total, (8, YR_DEV))
    msend[:, YR_DEV:] = jnp.zeros((8, LANES - YR_DEV), F32)

    def mean_copy(k):
        return pltpu.make_async_remote_copy(
            src_ref=msend,
            dst_ref=mrecv.at[k - 1],
            send_sem=m_send.at[k - 1],
            recv_sem=m_recv.at[k - 1],
            device_id={"loc": lax.rem(me + k, n_loc)},
            device_id_type=MESH,
        )

    for k in range(1, n_loc):
        mean_copy(k).start()

    for t in range(nz):
        sib_copy(t).wait_send()
    for tau in range(nz - 1):
        for c in range(chunks):

            @pl.when(z <= tau)
            def _():
                up(nz - 1 - tau + z, c).wait_send()

            @pl.when(nz - 1 - z <= tau)
            def _():
                down(tau - (nz - 1) + z, c).wait_send()

    for c in range(chunks):
        for k in range(1, n_ev):
            year_copy(c, k).wait_send()

    mean = msend[...]
    for k in range(1, n_loc):
        mean_copy(k).wait_recv()
        mean += mrecv[k - 1]
    mean_ref[...] = (mean / contracts)[:1, :YR_DEV]
    for k in range(1, n_loc):
        mean_copy(k).wait_send()


def solution(mesh):
    n_loc, n_ev = mesh.shape["loc"], mesh.shape["ev"]
    nz = n_loc // CORES

    def local(bins, frac, mask, contract, which, expo, curves, year, oret, olim, aret, alim):
        events, locs = bins.shape
        share = oret.shape[0] // n_loc
        chunk = min(share, LANES)
        chunks = share // chunk
        dma = pltpu.SemaphoreType.DMA
        pieces = pltpu.VMEM((nz, share, events), F32)
        lanes = lambda x: x.reshape(-1, LANES)
        annual, mean = pl.pallas_call(
            functools.partial(kernel, n_loc, n_ev),
            out_shape=(
                jax.ShapeDtypeStruct((share, YR_DEV), F32),
                jax.ShapeDtypeStruct((1, YR_DEV), F32),
            ),
            in_specs=[pl.BlockSpec(memory_space=pltpu.VMEM)] * 12,
            out_specs=(pl.BlockSpec(memory_space=pltpu.VMEM),) * 2,
            scratch_shapes=[
                pltpu.VMEM((locs, nz * events), BF16),
                pieces,
                pieces,
                pieces,
                pieces,
                pieces,
                pltpu.VMEM((chunks, n_ev, YR_DEV, chunk), F32),
                pltpu.VMEM((chunks, n_ev - 1, YR_DEV, chunk), F32),
                pltpu.VMEM((8, LANES), F32),
                pltpu.VMEM((n_loc - 1, 8, LANES), F32),
                dma((nz,)),
                dma((nz,)),
                dma((nz, chunks)),
                dma((nz, chunks)),
                dma((nz, chunks)),
                dma((nz, chunks)),
                dma((chunks, n_ev - 1)),
                dma((chunks, n_ev - 1)),
                dma((n_loc - 1,)),
                dma((n_loc - 1,)),
            ],
            compiler_params=pltpu.CompilerParams(
                collective_id=0, has_side_effects=True, vmem_limit_bytes=48 * 2**20
            ),
        )(
            bins,
            frac,
            mask,
            lanes(contract),
            lanes(which),
            lanes(expo),
            curves,
            lanes(year),
            lanes(oret),
            lanes(olim),
            lanes(aret),
            lanes(alim),
        )
        return annual, mean.reshape(YR_DEV)

    part = ("grp", "loc")
    in_specs = (
        P("ev", part),
        P("ev", part),
        P("ev", part),
        P(part),
        P(part),
        P(part),
        P(),
        P("ev"),
        P("grp"),
        P("grp"),
        P("grp"),
        P("grp"),
    )
    out_specs = (P(part, "ev"), P(("grp", "ev")))
    return jax.shard_map(local, mesh=mesh, in_specs=in_specs, out_specs=out_specs, check_vma=False)
```

time: 136 us -> 32.6 us (0.24)
  waiting for transfers between devices: 40.9 us -> 0 us
  other arithmetic: 34.6 us -> 0 us
  Pallas kernels: 0 us -> 26.2 us
  blocking collectives: 16.3 us -> 0 us
  between operations: 14.1 us -> 0.7 us
  matrix products: 12.6 us -> 0 us
  loops' own time: 5.83 us -> 0 us
  local copies, waits for them, and re-layouts: 9.98 us -> 5.39 us
    reduce_scatter x2 -> x0, waiting for transfers between devices: 40.9 us -> none  [the longest x1 33.6 us: local(): lax.psum_scatter(lax.map(one_piece, jnp.arange(pieces, dtype=jnp.int32))....]
    pallas_call x0 -> x1, Pallas kernels: none -> 26.2 us  [local(): pl.pallas_call(functools.partial(kernel, n_loc, n_ev), out_shape=(jax.Sha...]
    psum x1 -> x0, blocking collectives: 16.3 us -> none  [local(): year_mean = lax.psum(jnp.sum(annual, axis=0), 'loc') / contract_count]
    reduce_sum x9 -> x0, other arithmetic: 14.7 us -> none  [the longest x8 13.1 us: damage_rows(): damage = jnp.sum(hats * knot_table[None, :, :], axis=1)]
    dot_general x10 -> x0, matrix products: 12.6 us -> none  [the longest x8 9.5 us: one_piece(): lax.dot_general(member, loss, (((0,), (1,)), ((), ())), preferred_element...]
    dynamic_slice x20 -> x0, local copies, waits for them, and re-layouts: 7.78 us -> none  [the longest x8 4.66 us: local(): lax.map(one_piece, jnp.arange(pieces, dtype=jnp.int32))]
    add x16 -> x0, other arithmetic: 6.82 us -> none  [the longest x8 6.79 us: damage_rows(): bins_wide + 1 == knot_index]
    convert_element_type x16 -> x0, other arithmetic: 6.19 us -> none  [the longest x8 6.16 us: damage_rows(): weight = frac.astype(jnp.float32)[:, None, :]]
  transfers between devices with their start and end apart: 2 -> 0, of which waited for: 2 -> 0; matrix products, arithmetic and copies ran while one was open for 2% -> 0% of each run, Pallas kernels for 0% -> 0%
where the time goes in v1:
time: 32.6 us; the launch traced here: 32.3 us
  Pallas kernels  26.2 us (80%)
  local copies, waits for them, and re-layouts  5.39 us (17%)
  between operations  0.7 us (2%)
    pallas_call x1, Pallas kernels, local(): pl.pallas_call(functools.partial(kernel, n_loc, n_ev), out_shape=(jax.Sha...  26.2 us
    unnamed x28, local copies, waits for them, and re-layouts  5.39 us

profile of v1, /device:TPU:0, one launch (start us, length us, event | category | flops | bytes accessed | tf_op | source)
XLA Modules:
  0.0 32.3 jit_solution(3034556684726360650)
XLA Ops:
  0.6 0.0 copy-start.11
  0.6 0.7 %copy-done.11 = s32[128,8]{0,1:T(8,128)S(1)} copy-done((s32[128,8]{0,1:T(8,128)S(1)}, s32[128,8]{0,1:T(8,128)}, u32[]{:S(2)}) %copy-start.11) | copy-done | bytes 4120
  1.3 0.0 copy-start.10
  1.3 0.1 copy.14.mask_ref
  1.4 0.7 %copy-done.10 = f32[128,64]{0,1:T(8,128)S(1)} copy-done((f32[128,64]{0,1:T(8,128)S(1)}, f32[128,64]{0,1:T(8,128)}, u32[]{:S(2)}) %copy-start.10) | copy-done | bytes 32792
  2.1 0.0 copy-start.2
  2.1 0.0 copy-start.3
  2.1 0.0 copy-start.4
  2.1 0.0 copy-start.5
  2.1 0.0 copy-start.6
  2.1 0.0 copy-start.7
  2.1 0.0 copy-start.8
  2.1 0.0 copy-start.9
  2.1 0.1 copy.15.curves_ref
  2.2 0.5 %copy-done.2 = f32[2048]{0:T(1024)S(1)} copy-done((f32[2048]{0:T(1024)S(1)}, f32[2048]{0:T(1024)}, u32[]{:S(2)}) %copy-start.2) | copy-done | bytes 8216
  2.8 0.0 copy-done.3
  2.8 0.0 copy-done.4
  2.8 0.0 copy-done.5
  2.8 0.0 copy-done.6
  2.8 0.0 copy-done.7
  2.8 0.0 copy-done.8
  2.9 0.0 copy-done.9
  2.9 0.0 copy-start
  2.9 1.0 %copy-done = s32[128,1024]{1,0:T(8,128)S(1)} copy-done((s32[128,1024]{1,0:T(8,128)S(1)}, s32[128,1024]{1,0:T(8,128)}, u32[]{:S(2)}) %copy-start) | copy-done | bytes 524312
  3.9 0.0 copy-start.1
  3.9 0.9 %copy-done.1 = bf16[128,1024]{1,0:T(8,128)(2,1)S(1)} copy-done((bf16[128,1024]{1,0:T(8,128)(2,1)S(1)}, bf16[128,1024]{1,0:T(8,128)(2,1)}, u32[]{:S(2)}) %copy-start.1) | copy-done | bytes 262168
  4.9 26.2 %shard_map.131 = (f32[256,64]{1,0:T(8,128)S(1)}, f32[1,64]{1,0:T(1,128)S(1)}) custom-call(s32[128,1024]{1,0:T(8,128)S(1)} %copy-done, bf16[128,1024]{1,0:T(8,128)(2,1)S(1)} %copy-done.1, s32[128,8]{1,0:T(8,128)S(1)} %copy.14.mask_ref, s32[8,128]{1,0:T(8,128)S(1)} %bitcast.13, s32[8,128]{1,0:T(8,128)S(1)} %bitcast.14, f32[8,128]{1,0:T(8,128)S(1)} %bitcast.15, ...), custom_call_target="tpu_custom_call" | custom-call | tf_op jit(solution)/shard_map/pallas_call | solution.py:342
  31.0 0.7 %copy.16 = f32[256,64]{0,1:T(8,128)} copy(f32[256,64]{1,0:T(8,128)S(1)} %get-tuple-element.6) | data formatting | bytes 131072
  31.8 0.5 %copy.18 = f32[64]{0:T(128)} copy(f32[64]{0:T(128)S(1)} %bitcast.17) | data formatting | bytes 512
Async XLA Ops:
  0.6 0.7 %copy-start.11 = (s32[128,8]{0,1:T(8,128)S(1)}, s32[128,8]{0,1:T(8,128)}, u32[]{:S(2)}) copy-start(s32[128,8]{0,1:T(8,128)} %param.14) | copy-start | bytes 12292
  1.3 0.8 %copy-start.10 = (f32[128,64]{0,1:T(8,128)S(1)}, f32[128,64]{0,1:T(8,128)}, u32[]{:S(2)}) copy-start(f32[128,64]{0,1:T(8,128)} %param.18) | copy-start | bytes 98308
  2.1 0.7 %copy-start.2 = (f32[2048]{0:T(1024)S(1)}, f32[2048]{0:T(1024)}, u32[]{:S(2)}) copy-start(f32[2048]{0:T(1024)} %param.20) | copy-start | bytes 24580
  2.1 0.7 %copy-start.3 = (f32[2048]{0:T(1024)S(1)}, f32[2048]{0:T(1024)}, u32[]{:S(2)}) copy-start(f32[2048]{0:T(1024)} %param.21) | copy-start | bytes 24580
  2.1 0.7 %copy-start.4 = (f32[2048]{0:T(1024)S(1)}, f32[2048]{0:T(1024)}, u32[]{:S(2)}) copy-start(f32[2048]{0:T(1024)} %param.22) | copy-start | bytes 24580
  2.1 0.7 %copy-start.5 = (f32[2048]{0:T(1024)S(1)}, f32[2048]{0:T(1024)}, u32[]{:S(2)}) copy-start(f32[2048]{0:T(1024)} %param.23) | copy-start | bytes 24580
  2.1 0.7 %copy-start.6 = (s32[1024]{0:T(1024)S(1)}, s32[1024]{0:T(1024)}, u32[]{:S(2)}) copy-start(s32[1024]{0:T(1024)} %param.15) | copy-start | bytes 12292
  2.1 0.7 %copy-start.7 = (s32[1024]{0:T(1024)S(1)}, s32[1024]{0:T(1024)}, u32[]{:S(2)}) copy-start(s32[1024]{0:T(1024)} %param.16) | copy-start | bytes 12292
  2.1 0.7 %copy-start.8 = (f32[1024]{0:T(1024)S(1)}, f32[1024]{0:T(1024)}, u32[]{:S(2)}) copy-start(f32[1024]{0:T(1024)} %param.17) | copy-start | bytes 12292
  2.1 0.7 %copy-start.9 = (s32[128]{0:T(128)S(1)}, s32[128]{0:T(128)}, u32[]{:S(2)}) copy-start(s32[128]{0:T(128)} %param.19) | copy-start | bytes 1540
  2.9 1.0 %copy-start = (s32[128,1024]{1,0:T(8,128)S(1)}, s32[128,1024]{1,0:T(8,128)}, u32[]{:S(2)}) copy-start(s32[128,1024]{1,0:T(8,128)} %bins_ref.1) | copy-start | bytes 1572868
  3.9 0.9 %copy-start.1 = (bf16[128,1024]{1,0:T(8,128)(2,1)S(1)}, bf16[128,1024]{1,0:T(8,128)(2,1)}, u32[]{:S(2)}) copy-start(bf16[128,1024]{1,0:T(8,128)(2,1)} %frac_ref.1) | copy-start | bytes 786436

commit v2 on v1

--- a/solution.py
+++ b/solution.py
@@ -1,4 +1,5 @@
 import functools
+import math
 
 import jax
 import jax.numpy as jnp
@@ -29,6 +30,20 @@
 def kernel(
     n_loc,
     n_ev,
+    bins_hbm,
+    frac_hbm,
+    mask_hbm,
+    contract_hbm,
+    class_hbm,
+    expo_hbm,
+    curves_hbm,
+    year_hbm,
+    oret_hbm,
+    olim_hbm,
+    aret_hbm,
+    alim_hbm,
+    annual_ref,
+    mean_ref,
     bins_ref,
     frac_ref,
     mask_ref,
@@ -41,8 +56,8 @@
     olim_ref,
     aret_ref,
     alim_ref,
-    annual_ref,
-    mean_ref,
+    wide_sem,
+    small_sem,
     spread,
     psib,
     own,
@@ -66,10 +81,10 @@
 ):
     nz = n_loc // CORES
     events, locs = bins_ref.shape
-    blocks = mask_ref.shape[1]
+    blocks = mask_ref.shape[0]
     wide = locs // blocks
-    curve_count, knots = curves_ref.shape
-    share = annual_ref.shape[0]
+    knots, curve_count = curves_ref.shape
+    share = annual_ref.shape[1]
     chip = share * CORES
     contracts = share * n_loc
     chunk = ybuf.shape[3]
@@ -81,6 +96,39 @@
     other = 1 - core
     sibling = z * CORES + other
 
+    small = [
+        pltpu.make_async_copy(source, target, small_sem.at[i])
+        for i, (source, target) in enumerate(
+            (
+                (curves_hbm, curves_ref),
+                (class_hbm, class_ref),
+                (expo_hbm, expo_ref),
+                (contract_hbm, contract_ref),
+                (mask_hbm, mask_ref),
+                (year_hbm, year_ref),
+                (oret_hbm, oret_ref),
+                (olim_hbm, olim_ref),
+                (aret_hbm, aret_ref),
+                (alim_hbm, alim_ref),
+            )
+        )
+    ]
+    loads = wide_sem.shape[1]
+    load_cols = locs // loads
+    wides = [
+        [
+            pltpu.make_async_copy(
+                source.at[:, pl.ds(i * load_cols, load_cols)],
+                target.at[:, pl.ds(i * load_cols, load_cols)],
+                wide_sem.at[j, i],
+            )
+            for j, (source, target) in enumerate(((bins_hbm, bins_ref), (frac_hbm, frac_ref)))
+        ]
+        for i in range(loads)
+    ]
+    for copy in small[:5] + [copy for pair in wides for copy in pair] + small[5:]:
+        copy.start()
+
     barrier = pltpu.get_barrier_semaphore()
     for k in range(1, n_loc):
         pl.semaphore_signal(
@@ -91,11 +139,11 @@
             barrier, inc=1, device_id={"ev": lax.rem(ev + k, n_ev)}, device_id_type=MESH
         )
 
+    for copy in small[:5]:
+        copy.wait()
     curves = curves_ref[...]
-    steps = jnp.concatenate(
-        [curves[:, 1:] - curves[:, :-1], jnp.zeros((curve_count, 1), F32)], axis=1
-    )
-    c_high, c_low = split(jnp.concatenate([curves, steps], axis=1))
+    steps = jnp.concatenate([curves[1:] - curves[:-1], jnp.zeros((1, curve_count), F32)], axis=0)
+    c_high, c_low = split(jnp.concatenate([curves, steps], axis=0).T)
     blank = jnp.zeros((curve_count, LANES), BF16)
     first_row = (iota((16, LANES), 0) == 0).astype(F32).astype(BF16)
     table_rhs = jnp.concatenate(
@@ -105,13 +153,13 @@
         ],
         axis=1,
     )
-    eye = (iota((blocks, blocks), 0) == iota((blocks, blocks), 1)).astype(F32).astype(BF16)
-    keep = lax.dot_general(
-        eye, mask_ref[...].astype(F32).astype(BF16), NT, preferred_element_type=F32
-    )
+    keep = mask_ref[...].astype(F32)
     rows_in_chip = []
     for b in range(blocks):
         cols = pl.ds(b * wide, wide)
+        if b * wide % load_cols == 0:
+            for copy in wides[b * wide // load_cols]:
+                copy.wait()
         contract = contract_ref[b : b + 1, :]
         where_chip = jnp.zeros_like(contract)
         for t in range(1, nz):
@@ -170,6 +218,8 @@
     for t in range(nz):
         own[t] = sums[:, t * events : (t + 1) * events]
 
+    for copy in small[5:]:
+        copy.wait()
     first = me * share
 
     def row_of(ref, c):
@@ -281,9 +331,8 @@
         annual = jnp.minimum(
             jnp.maximum(yearly - row_of(aret_ref, c), 0.0), row_of(alim_ref, c)
         )
-        annual = annual.T
-        annual_ref[c * chunk : (c + 1) * chunk, :] = annual
-        total += jnp.sum(annual, axis=0, keepdims=True)
+        annual_ref[:, c * chunk : (c + 1) * chunk] = annual
+        total += jnp.sum(annual.T, axis=0, keepdims=True)
 
     msend[:, :YR_DEV] = jnp.broadcast_to(total, (8, YR_DEV))
     msend[:, YR_DEV:] = jnp.zeros((8, LANES - YR_DEV), F32)
@@ -339,15 +388,32 @@
         dma = pltpu.SemaphoreType.DMA
         pieces = pltpu.VMEM((nz, share, events), F32)
         lanes = lambda x: x.reshape(-1, LANES)
+        arguments = (
+            bins,
+            frac,
+            mask.T,
+            lanes(contract),
+            lanes(which),
+            lanes(expo),
+            curves.T,
+            lanes(year),
+            lanes(oret),
+            lanes(olim),
+            lanes(aret),
+            lanes(alim),
+        )
         annual, mean = pl.pallas_call(
             functools.partial(kernel, n_loc, n_ev),
             out_shape=(
-                jax.ShapeDtypeStruct((share, YR_DEV), F32),
+                jax.ShapeDtypeStruct((YR_DEV, share), F32),
                 jax.ShapeDtypeStruct((1, YR_DEV), F32),
             ),
-            in_specs=[pl.BlockSpec(memory_space=pltpu.VMEM)] * 12,
+            in_specs=[pl.BlockSpec(memory_space=pltpu.HBM)] * 12,
             out_specs=(pl.BlockSpec(memory_space=pltpu.VMEM),) * 2,
-            scratch_shapes=[
+            scratch_shapes=[pltpu.VMEM(x.shape, x.dtype) for x in arguments]
+            + [
+                dma((2, math.gcd(mask.shape[1], 4))),
+                dma((10,)),
                 pltpu.VMEM((locs, nz * events), BF16),
                 pieces,
                 pieces,
@@ -370,23 +436,10 @@
                 dma((n_loc - 1,)),
             ],
             compiler_params=pltpu.CompilerParams(
-                collective_id=0, has_side_effects=True, vmem_limit_bytes=48 * 2**20
+                collective_id=0, has_side_effects=True, vmem_limit_bytes=60 * 2**20
             ),
-        )(
-            bins,
-            frac,
-            mask,
-            lanes(contract),
-            lanes(which),
-            lanes(expo),
-            curves,
-            lanes(year),
-            lanes(oret),
-            lanes(olim),
-            lanes(aret),
-            lanes(alim),
-        )
-        return annual, mean.reshape(YR_DEV)
+        )(*arguments)
+        return annual.T, mean.reshape(YR_DEV)
 
     part = ("grp", "loc")
     in_specs = (

time: 32.6 us -> 29.9 us (0.917)
  local copies, waits for them, and re-layouts: 5.39 us -> 1.99 us
  Pallas kernels: 26.2 us -> 27 us
    unnamed x28 -> x4, local copies, waits for them, and re-layouts: 5.39 us -> 1.99 us
    pallas_call x1, Pallas kernels: 26.2 us -> 27 us  [local(): pl.pallas_call(functools.partial(kernel, n_loc, n_ev), out_shape=(jax.Sha...]
where the time goes in v2:
time: 29.9 us; the launch traced here: 29.7 us
  Pallas kernels  27 us (90%)
  local copies, waits for them, and re-layouts  1.99 us (7%)
  between operations  0.65 us (2%)
    pallas_call x1, Pallas kernels, local(): pl.pallas_call(functools.partial(kernel, n_loc, n_ev), out_shape=(jax.Sha...  27 us
    unnamed x4, local copies, waits for them, and re-layouts  1.99 us

profile of v2, /device:TPU:0, one launch (start us, length us, event | category | flops | bytes accessed | tf_op | source)
XLA Modules:
  0.0 29.7 jit_solution(4775188034544520704)
XLA Ops:
  0.6 27.0 %shard_map.131 = (f32[64,256]{1,0:T(8,128)}, f32[1,64]{1,0:T(1,128)}) custom-call(s32[128,1024]{1,0:T(8,128)} %bins_hbm.1, bf16[128,1024]{1,0:T(8,128)(2,1)} %frac_hbm.1, s32[8,128]{1,0:T(8,128)} %bitcast.18, s32[8,128]{1,0:T(8,128)} %bitcast.19, s32[8,128]{1,0:T(8,128)} %bitcast.20, f32[8,128]{1,0:T(8,128)} %bitcast.21, f32[64,128]{1,0:T(8,128)} %bitcast.13, ...), custom_call_target="tpu_custom_call" | custom-call | tf_op jit(solution)/shard_map/pallas_call | solution.py:405
  27.7 0.0 copy-start
  27.7 1.5 %copy.16 = f32[256,64]{0,1:T(8,128)} copy(f32[256,64]{0,1:T(8,128)} %bitcast.12) | data formatting | bytes 131072
  29.2 0.0 copy-done
  29.2 0.5 %copy.17 = f32[64]{0:T(128)} copy(f32[64]{0:T(128)S(1)} %bitcast.23) | data formatting | bytes 512
Async XLA Ops:
  27.7 1.5 %copy-start = (f32[1,64]{1,0:T(1,128)S(1)}, f32[1,64]{1,0:T(1,128)}, u32[]{:S(2)}) copy-start(f32[1,64]{1,0:T(1,128)} %get-tuple-element.5) | copy-start | bytes 772

commit v3 on v2

--- a/solution.py
+++ b/solution.py
@@ -89,6 +89,8 @@
     contracts = share * n_loc
     chunk = ybuf.shape[3]
     chunks = share // chunk
+    parts = up_send.shape[1]
+    part = share // parts
 
     me = lax.axis_index("loc")
     ev = lax.axis_index("ev")
@@ -175,10 +177,10 @@
         table, home = both[:, :LANES], both[:, LANES:]
         place = (bins_ref[:, cols].astype(F32) + frac_ref[:, cols].astype(F32)).T
         knot = place.astype(I32)
-        part = place - knot.astype(F32)
+        rest = place - knot.astype(F32)
         low = jnp.take_along_axis(table, knot, axis=1, mode="promise_in_bounds")
         rise = jnp.take_along_axis(table, knot + knots, axis=1, mode="promise_in_bounds")
-        loss = (low + part * rise) * keep[b : b + 1, :]
+        loss = (low + rest * rise) * keep[b : b + 1, :]
         for t in range(nz):
             spread[cols, pl.ds(t * events, events)] = jnp.where(home == t, loss, 0.0).astype(BF16)
 
@@ -195,6 +197,36 @@
     sums = partial(other)
     for t in range(nz):
         psib[t] = sums[:, t * events : (t + 1) * events]
+
+    sums = partial(core)
+    for t in range(nz):
+        own[t] = sums[:, t * events : (t + 1) * events]
+
+    for copy in small[5:]:
+        copy.wait()
+    first = me * share
+
+    def row_of(ref, c):
+        start = first + c * chunk
+        row = ref[pl.ds(start // LANES, 1), :]
+        if share % LANES:
+            row = pltpu.roll(
+                jnp.broadcast_to(row, (8, LANES)), (LANES - start % LANES) % LANES, 1
+            )[:1]
+        return row[:, :chunk]
+
+    def column_of(ref, c):
+        row = jnp.broadcast_to(row_of(ref, c), (chunk, chunk))
+        return jnp.sum(
+            jnp.where(iota((chunk, chunk), 0) == iota((chunk, chunk), 1), row, 0.0),
+            axis=1,
+            keepdims=True,
+        )
+
+    orets = [column_of(oret_ref, c) for c in range(chunks)]
+    olims = [column_of(olim_ref, c) for c in range(chunks)]
+    year_rows = (iota((n_ev * YR_DEV, events), 0) == year_ref[...]).astype(F32).astype(BF16)
+    year_rows = jnp.concatenate([year_rows, year_rows], axis=1)
 
     pl.semaphore_wait(barrier, n_loc - 1 + n_ev - 1)
 
@@ -208,44 +240,12 @@
             device_id_type=MESH,
         )
 
-    order = []
-    for t in range((nz + 1) // 2):
-        order += [t] if t == nz - 1 - t else [nz - 1 - t, t]
-    for t in order:
-        sib_copy(t).start()
-
-    sums = partial(core)
-    for t in range(nz):
-        own[t] = sums[:, t * events : (t + 1) * events]
-
-    for copy in small[5:]:
-        copy.wait()
-    first = me * share
-
-    def row_of(ref, c):
-        start = first + c * chunk
-        row = ref[pl.ds(start // LANES, 1), :]
-        if share % LANES:
-            row = pltpu.roll(
-                jnp.broadcast_to(row, (8, LANES)), (LANES - start % LANES) % LANES, 1
-            )[:1]
-        return row[:, :chunk]
-
-    def column_of(ref, c):
-        row = jnp.broadcast_to(row_of(ref, c), (chunk, chunk))
-        return jnp.sum(
-            jnp.where(iota((chunk, chunk), 0) == iota((chunk, chunk), 1), row, 0.0),
-            axis=1,
-            keepdims=True,
-        )
-
-    orets = [column_of(oret_ref, c) for c in range(chunks)]
-    olims = [column_of(olim_ref, c) for c in range(chunks)]
-    year_rows = (iota((n_ev * YR_DEV, events), 0) == year_ref[...]).astype(F32).astype(BF16)
-    year_rows = jnp.concatenate([year_rows, year_rows], axis=1)
+    lower = (z < nz // 2).astype(I32)
+    for i in range(nz):
+        sib_copy(i + lower * (nz - 1 - 2 * i)).start()
 
     def hop(t, c, send, recv, into, step):
-        rows = pl.ds(c * chunk, chunk)
+        rows = pl.ds(c * part, part)
         return pltpu.make_async_remote_copy(
             src_ref=own.at[t, rows],
             dst_ref=into.at[t, rows],
@@ -259,7 +259,7 @@
     down = functools.partial(hop, send=dn_send, recv=dn_recv, into=dnr, step=-CORES)
 
     def pass_on(t, c, way, into, inner):
-        rows = pl.ds(c * chunk, chunk)
+        rows = pl.ds(c * part, part)
         if c == 0:
             sib_copy(t).wait_recv()
 
@@ -275,7 +275,7 @@
         way(t, c).start()
 
     for tau in range(nz - 1):
-        for c in range(chunks):
+        for c in range(parts):
 
             @pl.when(z <= tau)
             def _():
@@ -299,15 +299,18 @@
     for c in range(chunks):
         rows = pl.ds(c * chunk, chunk)
         own[z, rows] = own[z, rows] + sibr[z, rows]
+        arrived = range(c * parts // chunks, (c + 1) * parts // chunks)
 
         @pl.when(z > 0)
         def _():
-            up(z, c).wait_recv()
+            for p in arrived:
+                up(z, p).wait_recv()
             own[z, rows] = own[z, rows] + upr[z, rows]
 
         @pl.when(z < nz - 1)
         def _():
-            down(z, c).wait_recv()
+            for p in arrived:
+                down(z, p).wait_recv()
             own[z, rows] = own[z, rows] + dnr[z, rows]
 
         occurrence = jnp.minimum(jnp.maximum(own[z, rows] - orets[c], 0.0), olims[c])
@@ -353,7 +356,7 @@
     for t in range(nz):
         sib_copy(t).wait_send()
     for tau in range(nz - 1):
-        for c in range(chunks):
+        for c in range(parts):
 
             @pl.when(z <= tau)
             def _():
@@ -426,10 +429,10 @@
                 pltpu.VMEM((n_loc - 1, 8, LANES), F32),
                 dma((nz,)),
                 dma((nz,)),
-                dma((nz, chunks)),
-                dma((nz, chunks)),
-                dma((nz, chunks)),
-                dma((nz, chunks)),
+                dma((nz, 2 * chunks)),
+                dma((nz, 2 * chunks)),
+                dma((nz, 2 * chunks)),
+                dma((nz, 2 * chunks)),
                 dma((chunks, n_ev - 1)),
                 dma((chunks, n_ev - 1)),
                 dma((n_loc - 1,)),
@@ -439,7 +442,7 @@
                 collective_id=0, has_side_effects=True, vmem_limit_bytes=60 * 2**20
             ),
         )(*arguments)
-        return annual.T, mean.reshape(YR_DEV)
+        return jnp.maximum(annual.T, 0.0), mean.reshape(YR_DEV)
 
     part = ("grp", "loc")
     in_specs = (

time: 29.9 us -> 30.1 us (level)
  other arithmetic: 0 us -> 1.47 us
  local copies, waits for them, and re-layouts: 1.99 us -> 1.11 us
  Pallas kernels: 27 us -> 26.6 us
    max x0 -> x1, other arithmetic: none -> 1.47 us  [local(): return (jnp.maximum(annual.T, 0.0), mean.reshape(YR_DEV))]
    unnamed x4 -> x3, local copies, waits for them, and re-layouts: 1.99 us -> 1.11 us
    pallas_call x1, Pallas kernels: 27 us -> 26.6 us  [local(): pl.pallas_call(functools.partial(kernel, n_loc, n_ev), out_shape=(jax.Sha...]
where the time goes in v3:
time: 30.1 us; the launch traced here: 29.9 us
  Pallas kernels  26.6 us (88%)
  other arithmetic  1.47 us (5%)
  local copies, waits for them, and re-layouts  1.11 us (4%)
  between operations  0.64 us (2%)
    pallas_call x1, Pallas kernels, local(): pl.pallas_call(functools.partial(kernel, n_loc, n_ev), out_shape=(jax.Sha...  26.6 us
    max x1, other arithmetic, local(): return (jnp.maximum(annual.T, 0.0), mean.reshape(YR_DEV))  1.47 us
    unnamed x3, local copies, waits for them, and re-layouts  1.11 us

profile of v3, /device:TPU:0, one launch (start us, length us, event | category | flops | bytes accessed | tf_op | source)
XLA Modules:
  0.0 29.9 jit_solution(758969157508147969)
XLA Ops:
  0.6 26.6 %shard_map.131 = (f32[64,256]{1,0:T(8,128)}, f32[1,64]{1,0:T(1,128)}) custom-call(s32[128,1024]{1,0:T(8,128)} %bins_hbm.1, bf16[128,1024]{1,0:T(8,128)(2,1)} %frac_hbm.1, s32[8,128]{1,0:T(8,128)} %bitcast.18, s32[8,128]{1,0:T(8,128)} %bitcast.19, s32[8,128]{1,0:T(8,128)} %bitcast.20, f32[8,128]{1,0:T(8,128)} %bitcast.21, f32[64,128]{1,0:T(8,128)} %bitcast.13, ...), custom_call_target="tpu_custom_call" | custom-call | tf_op jit(solution)/shard_map/pallas_call | solution.py:408
  27.3 1.5 %maximum_bitcast_fusion = f32[256,64]{0,1:T(8,128)} fusion(f32[64,256]{1,0:T(8,128)} %get-tuple-element.4), kind=kLoop, calls=%fused_computation | loop fusion | flops 16384 | bytes 131072 | tf_op jit(solution)/shard_map/max | solution.py:445
  28.8 0.0 copy-start
  28.8 0.6 %copy-done = f32[1,64]{1,0:T(1,128)S(1)} copy-done((f32[1,64]{1,0:T(1,128)S(1)}, f32[1,64]{1,0:T(1,128)}, u32[]{:S(2)}) %copy-start) | copy-done | bytes 280
  29.4 0.5 %copy.15 = f32[64]{0:T(128)} copy(f32[64]{0:T(128)S(1)} %bitcast.23) | data formatting | bytes 512
Async XLA Ops:
  28.8 0.6 %copy-start = (f32[1,64]{1,0:T(1,128)S(1)}, f32[1,64]{1,0:T(1,128)}, u32[]{:S(2)}) copy-start(f32[1,64]{1,0:T(1,128)} %get-tuple-element.5) | copy-start | bytes 772
